TPU v7x, 32 devices: a whole 2x2x4 slice. The times are simulated.
32 devices in a mesh: wide: 8 (over z, core), narrow: 4 (over y, x).
Axes of the slice: x: 2, y: 2, z: 4, core: 2. Of those that a mesh axis runs over, the one named last changes fastest.
Arguments:
- state: float32 [2, 4194304], P(None, ('wide', 'narrow')), may hold values from -6 to 6
- gates: float32 [4, 2, 128, 128], replicated, may hold values from -0.375 to 0.375
- phase_index: int32 [3, 128], replicated, may hold values from 0 to 255
Outputs:
- final_state: float32 [2, 4194304], P(None, ('wide', 'narrow'))
All inputs are finite; a program needn't handle non-finite values.
Results may differ from a plain program's by a relative error of at most 0.00007.
Values sent between devices are 32-bit elements; how exact they have to be, the bound alone decides.
A program may use at most 64 MiB of HBM per device.

v0:
```python
import math

import jax
import jax.numpy as jnp
from jax import lax
from jax.sharding import PartitionSpec as P

GATE = 128


angle_step = 2.0 * math.pi / 256.0


def swapped(value, axis, distance):
    mask = 2**distance
    pairs = [(source, source ^ mask) for source in range(lax.axis_size(axis))]
    return lax.ppermute(value, axis, pairs)


def real_form(gate_re, gate_im):
    upper = jnp.stack([gate_re, -gate_im], axis=1)
    lower = jnp.stack([gate_im, gate_re], axis=1)
    return jnp.stack([upper, lower], axis=0)


def apply_last(blocks, amplitudes):
    return jnp.einsum("pmqn,qrn->prm", blocks, amplitudes, precision=lax.Precision.HIGHEST)


def apply_middle(blocks, amplitudes):
    return jnp.einsum("pmqn,qbnc->pbmc", blocks, amplitudes, precision=lax.Precision.HIGHEST)


def apply_front(blocks, amplitudes):
    return jnp.einsum("pmqn,qnk->pmk", blocks, amplitudes, precision=lax.Precision.HIGHEST)


def rotate(amplitudes, angle_sum):
    angles = angle_sum.astype(jnp.float32) * angle_step
    cosine = jnp.cos(angles)
    sine = jnp.sin(angles)
    real_part = amplitudes[0] * cosine - amplitudes[1] * sine
    imag_part = amplitudes[0] * sine + amplitudes[1] * cosine
    return jnp.stack([real_part, imag_part], axis=0)


def local(state, gates, phase_index):
    local_amps = state.shape[1]
    narrow_count = lax.axis_size("narrow")
    wide_count = lax.axis_size("wide")
    top_bit = wide_count.bit_length() - 2
    wide_bit = lax.axis_index("wide") // (wide_count // 2)
    device = lax.axis_index("wide") * narrow_count + lax.axis_index("narrow")
    half_gate = GATE // 2
    row_count = local_amps // GATE
    amps = apply_last(real_form(gates[0, 0], gates[0, 1]), state.reshape(2, row_count, GATE))
    amps = apply_middle(
        real_form(gates[1, 0], gates[1, 1]),
        amps.reshape(2, local_amps // (GATE * GATE), GATE, GATE),
    )
    span_rows = local_amps * wide_count * narrow_count // (GATE * GATE)
    row_ids = device * row_count + lax.iota(jnp.int32, row_count)
    middle_part = jnp.tile(phase_index[1], row_count // GATE)
    top_ids = row_ids // span_rows
    one_hot = top_ids[:, None] == lax.iota(jnp.int32, GATE)[None, :]
    top_part = jnp.sum(jnp.where(one_hot, phase_index[2][None, :], 0), axis=1)
    angle_sum = phase_index[0][None, :] + (middle_part + top_part)[:, None]
    amps = rotate(amps.reshape(2, row_count, GATE), angle_sum)
    third = real_form(gates[2, 0], gates[2, 1])
    fourth = real_form(gates[3, 0], gates[3, 1])
    laid_out = amps.reshape(2, narrow_count, GATE // narrow_count, local_amps // GATE)
    portion = lax.all_to_all(laid_out, "narrow", split_axis=1, concat_axis=1, tiled=True)
    columns = portion.shape[3]
    current = apply_front(third, portion.reshape(2, GATE, columns)).reshape(
        2, 2, half_gate, columns
    )
    received = swapped(current, "wide", top_bit)
    row_sel = lax.dynamic_slice_in_dim(fourth, wide_bit * half_gate, half_gate, 1)
    row_blocks = row_sel.reshape(2, half_gate, 2, 2, half_gate)
    own_block = lax.dynamic_index_in_dim(row_blocks, wide_bit, 3, keepdims=False)
    partner_block = lax.dynamic_index_in_dim(row_blocks, 1 - wide_bit, 3, keepdims=False)
    pair_blocks = jnp.stack([own_block, partner_block], axis=3)
    inputs = jnp.stack([current, received], axis=1)
    current = jnp.einsum("omisn,istnk->otmk", pair_blocks, inputs, precision=lax.Precision.HIGHEST)
    current = current.reshape(2, narrow_count, GATE // narrow_count, columns)
    result = lax.all_to_all(current, "narrow", split_axis=1, concat_axis=1, tiled=True)
    return result.reshape(2, local_amps)


def solution(mesh):
    in_specs = (P(None, ("wide", "narrow")), P(), P())
    out_specs = P(None, ("wide", "narrow"))
    return jax.shard_map(local, mesh=mesh, in_specs=in_specs, out_specs=out_specs, check_vma=False)
```

profile of v0, /device:TPU:0, one launch (start us, length us, event | category | flops | bytes accessed | tf_op | source)
XLA Modules:
  0.0 95.8 jit_solution(555099521380523418)
XLA Ops:
  0.0 0.0 copy-start
  0.0 0.0 copy-start.1
  0.0 1.2 %slice_bitcast_fusion = (f32[128,1,128]{2,0,1:T(8,128)S(1)}, f32[128,1,128]{2,0,1:T(8,128)S(1)}, f32[128,1,128]{2,0,1:T(8,128)S(1)}, f32[128,1,128]{2,0,1:T(8,12...) fusion(f32[4,2,128,128]{3,2,1,0:T(8,128)} %param.4), kind=kLoop, calls=%fused_computation.42 | loop fusion | bytes 1048576 | tf_op jit(solution)/shard_map/squeeze | solution.py:70
  1.2 0.1 copy-done
  1.4 0.3 copy-done.1
  1.6 1.1 %fusion.4 = f32[2,128,1024,1]{2,1,3,0:T(8,128)S(1)} fusion(f32[1,2,1024,128]{3,1,2,0:T(2,128)S(1)} %bitcast.126, f32[1,128,2,128]{3,1,2,0:T(8,128)S(1)} %get-tuple-element.30, f32[1,128,2,128]{3,1,2,0:T(8,128)S(1)} %get-tuple-element.29), kind=kOutput, calls=%fused_computation.6 | convolution fusion | flops 805371904 | bytes 2359296 | tf_op jit(solution)/shard_map/pmqn,qrn->prm/dot_general | solution.py:27
  2.7 0.2 copy.61
  2.9 1.0 %convolution_bitcast_fusion = f32[2,8,128,128]{2,3,0,1:T(8,128)S(1)} fusion(f32[2,8,128,128,1]{2,1,3,0,4:T(8,128)S(1)} %bitcast.121, f32[1,128,2,128]{3,1,2,0:T(8,128)S(1)} %get-tuple-element.34, f32[1,128,2,128]{3,1,2,0:T(8,128)S(1)} %get-tuple-element.35), kind=kOutput, calls=%fused_computation.5 | convolution fusion | flops 805371904 | bytes 2359296 | tf_op jit(solution)/shard_map/pmqn,qbnc->pbmc/dot_general | solution.py:31
  4.0 0.1 fusion.33
  4.0 0.2 copy.39
  4.2 0.1 squeeze.26
  4.3 0.0 copy-start.2
  4.3 0.2 copy.40
  4.6 0.1 squeeze.27
  4.7 0.4 copy-done.2
  5.0 0.4 select_reduce_fusion
  5.4 0.2 add.90
  5.6 0.1 add.91
  5.7 2.1 %multiply_subtract_fusion = (f32[1,4,32,1024]{3,2,1,0:T(8,128)S(1)}, f32[1,4,32,1024]{3,2,1,0:T(8,128)S(1)}) fusion(f32[1,4,32,1024]{3,2,1,0:T(8,128)S(1)} %squeeze.27, f32[1,4,32,1024]{3,2,1,0:T(8,128)S(1)} %squeeze.26, s32[1,4,32,1024]{3,2,1,0:T(8,128)S(1)} %add.91, s32[1024]{0:T(1024)S(1)} %broadcast_bitcast_fusion), kind=kLoop, calls=%fused_computation.12 | loop fusion | flops 1179648 | bytes 2625536 | tf_op jit(solution)/shard_map/sub | solution.py:42
  7.8 0.1 pad_maximum_fusion
  7.9 1.1 %copy.41 = f32[2,4,32,1024]{3,2,0,1:T(8,128)} copy(f32[2,4,32,1024]{3,2,1,0:T(8,128)S(1)} %pad_maximum_fusion) | data formatting | bytes 2097152 | tf_op jit(solution)/shard_map/stack | solution.py:44
  9.0 5.2 %all-to-all-start = ((f32[2,4,32,1024]{3,2,0,1:T(8,128)}), f32[2,4,32,1024]{3,2,0,1:T(8,128)S(1)}, u32[]{:S(2)}, u32[]{:S(2)}) async-start(f32[2,4,32,1024]{3,2,0,1:T(8,128)} %copy.41), calls=%async_computation | async-start | bytes 2097152 | tf_op jit(solution)/shard_map/all_to_all | solution.py:72
  14.2 13.6 %all-to-all-done = f32[2,4,32,1024]{3,2,0,1:T(8,128)S(1)} async-done(((f32[2,4,32,1024]{3,2,0,1:T(8,128)}), f32[2,4,32,1024]{3,2,0,1:T(8,128)S(1)}, u32[]{:S(2)}, u32[]{:S(2)}) %all-to-all-start) | async-done | bytes 1048608 | tf_op jit(solution)/shard_map/all_to_all | solution.py:72
  27.8 0.1 copy.42
  27.9 1.0 %fusion.10 = f32[2,128,1024,1]{2,1,3,0:T(8,128)S(1)} fusion(f32[2,128,1024,1]{2,1,0,3:T(8,128)S(1)} %bitcast.122, f32[1,128,2,128]{3,1,2,0:T(8,128)S(1)} %get-tuple-element.26, f32[1,128,2,128]{3,1,2,0:T(8,128)S(1)} %get-tuple-element.25), kind=kOutput, calls=%fused_computation.18 | convolution fusion | flops 805371904 | bytes 2359296 | tf_op jit(solution)/shard_map/pmqn,qnk->pmk/dot_general | solution.py:35
  28.9 0.1 copy.43
  29.0 2.7 %collective-permute-start = (f32[2,2,64,1024]{3,2,0,1:T(8,128)S(1)}, f32[2,2,64,1024]{3,2,0,1:T(8,128)S(1)}, u32[]{:S(2)}, u32[]{:S(2)}) collective-permute-start(f32[2,2,64,1024]{3,2,0,1:T(8,128)S(1)} %copy.43), channel_id=1, source_target_pairs={{0,16},{4,20},{8,24},{12,28},{16,0},{20,4},{24,8},{28,12},{1,17},{... | collective-permute-start | bytes 3145736 | tf_op jit(solution)/shard_map/ppermute | solution.py:17
  31.8 0.2 reshape.203
  32.0 0.2 constant_dynamic-slice_fusion
  32.2 44.3 %collective-permute-done = f32[2,2,64,1024]{3,2,0,1:T(8,128)S(1)} collective-permute-done((f32[2,2,64,1024]{3,2,0,1:T(8,128)S(1)}, f32[2,2,64,1024]{3,2,0,1:T(8,128)S(1)}, u32[]{:S(2)}, u32[]{:S(2)}) %collective-permute-start) | collective-permute-done | bytes 1048608 | tf_op jit(solution)/shard_map/ppermute | solution.py:17
  76.5 1.3 %fusion.3 = f32[2,2,64,1024]{3,2,0,1:T(8,128)S(1)} fusion(f32[2,1,2,64,1024]{4,3,1,0,2:T(8,128)S(1)} %bitcast.127, f32[2,64,2,1,64]{4,1,3,2,0:T(8,128)S(1)} %bitcast.129, f32[2,64,2,1,64]{4,1,3,2,0:T(8,128)S(1)} %bitcast.128, f32[2,1,2,64,1024]{4,3,2,0,1:T(8,128)S(1)} %bitcast.120), kind=kOutput, calls=%fused_computation.4 | convolution fusion | flops 805863424 | bytes 3276800 | tf_op jit(solution)/shard_map/omisn,istnk->otmk/dot_general | solution.py:84
  77.9 0.1 copy.47
  78.0 0.1 copy.48
  78.1 15.9 %all_to_all.10 = f32[2,4,32,1024]{3,2,0,1:T(8,128)S(1)} all-to-all(f32[2,4,32,1024]{3,2,0,1:T(8,128)S(1)} %copy.48), channel_id=1, replica_groups=mesh['wide'=8,'narrow'=4] {'narrow'}, dimensions={1} | all-to-all | bytes 2097152 | tf_op jit(solution)/shard_map/all_to_all | solution.py:86
  94.0 0.1 copy.49
  94.0 1.8 %copy.62 = f32[1,2,128,1024]{3,1,2,0:T(2,128)} copy(f32[1,2,128,1024]{3,2,1,0:T(8,128)S(1)} %bitcast.125) | data formatting | bytes 2097152
  (9 shorter events, 0.1 us)
Async XLA Ops:
  0.0 1.3 %copy-start = (f32[4,2,128,128]{3,2,1,0:T(8,128)S(1)}, f32[4,2,128,128]{3,2,1,0:T(8,128)}, u32[]{:S(2)}) copy-start(f32[4,2,128,128]{3,2,1,0:T(8,128)} %param.4) | copy-start | bytes 1572868
  0.0 1.6 %copy-start.1 = (f32[2,131072]{1,0:T(2,128)S(1)}, f32[2,131072]{1,0:T(2,128)}, u32[]{:S(2)}) copy-start(f32[2,131072]{1,0:T(2,128)} %param.3) | copy-start | bytes 3145732
  4.3 0.7 copy-start.2
  9.0 18.8 %all-to-all-start = ((f32[2,4,32,1024]{3,2,0,1:T(8,128)}), f32[2,4,32,1024]{3,2,0,1:T(8,128)S(1)}, u32[]{:S(2)}, u32[]{:S(2)}) async-start(f32[2,4,32,1024]{3,2,0,1:T(8,128)} %copy.41), calls=%async_computation | async-start | bytes 2097152 | tf_op jit(solution)/shard_map/all_to_all | solution.py:72
  29.0 47.5 %collective-permute-start = (f32[2,2,64,1024]{3,2,0,1:T(8,128)S(1)}, f32[2,2,64,1024]{3,2,0,1:T(8,128)S(1)}, u32[]{:S(2)}, u32[]{:S(2)}) collective-permute-start(f32[2,2,64,1024]{3,2,0,1:T(8,128)S(1)} %copy.43), channel_id=1, source_target_pairs={{0,16},{4,20},{8,24},{12,28},{16,0},{20,4},{24,8},{28,12},{1,17},{... | collective-permute-start | bytes 3145736 | tf_op jit(solution)/shard_map/ppermute | solution.py:17
where the time goes:
time: 96.1 us; the launch traced here: 95.8 us
  waiting for transfers between devices  57.9 us (60%)
  blocking collectives  15.9 us (17%)
  starting transfers between devices  7.87 us (8%)
  local copies, waits for them, and re-layouts  6.74 us (7%)
  matrix products  4.48 us (5%)
  other arithmetic  2.67 us (3%)
    ppermute x1, waiting for transfers between devices, swapped(): return lax.ppermute(value, axis, pairs)  44.3 us
    all_to_all x1, blocking collectives, local(): lax.all_to_all(current, 'narrow', split_axis=1, concat_axis=1, tiled=True)  15.9 us
    all_to_all x1, waiting for transfers between devices, local(): lax.all_to_all(laid_out, 'narrow', split_axis=1, concat_axis=1, tiled=True)  13.6 us
    all_to_all x1, starting transfers between devices, local(): lax.all_to_all(laid_out, 'narrow', split_axis=1, concat_axis=1, tiled=True)  5.16 us
    ppermute x1, starting transfers between devices, swapped(): return lax.ppermute(value, axis, pairs)  2.71 us
    unnamed x8, local copies, waits for them, and re-layouts  2.68 us
    sub x1, other arithmetic, rotate(): real_part = amplitudes[0] * cosine - amplitudes[1] * sine  2.08 us
  transfers between devices with their start and end apart: 2, of which 2 were waited for; matrix products, arithmetic and copies ran while one was open for 1% of the time, Pallas kernels for 0%

commit v1 on v0

v1 whole, which is shorter than its diff:
```python
import functools
import math

import jax
import jax.numpy as jnp
from jax import lax
from jax.experimental import pallas as pl
from jax.experimental.pallas import tpu as pltpu
from jax.sharding import PartitionSpec as P

GATE = 128

angle_step = 2.0 * math.pi / 256.0


def split(value):
    high = value.astype(jnp.bfloat16)
    low = (value - high.astype(jnp.float32)).astype(jnp.bfloat16)
    return high, low


def product(left, right):
    (left_high, left_low), (right_high, right_low) = left, right
    dot = functools.partial(jnp.dot, preferred_element_type=jnp.float32)
    return dot(left_high, right_high) + (dot(left_high, right_low) + dot(left_low, right_high))


def real_form(gate_re, gate_im):
    upper = jnp.concatenate([gate_re, -gate_im], axis=1)
    lower = jnp.concatenate([gate_im, gate_re], axis=1)
    return jnp.concatenate([upper, lower], axis=0)


def kernel(
    dims,
    x_ref,
    gates_ref,
    phase_ref,
    out_ref,
    amps,
    gate_rows,
    spread,
    gathered,
    finished,
    returned,
    own_sem,
    swap_send,
    swap_recv,
    spread_send,
    spread_recv,
    return_send,
    return_recv,
):
    wide_count, narrow_count, chunk_count, free, extra, inner, low, per_dest, top_span = dims
    wide = lax.axis_index("wide")
    me = lax.axis_index("narrow")
    side = wide // (wide_count // 2)
    partner = lax.rem(wide + wide_count // 2, wide_count)
    sides = (wide, partner)
    half = GATE // 2

    def swap(c):
        return pltpu.make_async_remote_copy(
            src_ref=x_ref.at[1 - side, c],
            dst_ref=amps.at[1, c],
            send_sem=swap_send.at[c],
            recv_sem=swap_recv.at[c],
            device_id=(partner, me),
            device_id_type=pl.DeviceIdType.MESH,
        )

    def spread_copy(slot, f, d):
        dest = lax.rem(me + d, narrow_count)
        return pltpu.make_async_remote_copy(
            src_ref=spread.at[slot, f, dest],
            dst_ref=gathered.at[slot, f, me],
            send_sem=spread_send.at[slot, f, d],
            recv_sem=spread_recv.at[slot, f, me],
            device_id=(wide, dest),
            device_id_type=pl.DeviceIdType.MESH,
        )

    def spread_arrival(slot, f, d):
        source = lax.rem(me + d, narrow_count)
        return pltpu.make_async_remote_copy(
            src_ref=spread.at[slot, f, source],
            dst_ref=gathered.at[slot, f, source],
            send_sem=spread_send.at[slot, f, d],
            recv_sem=spread_recv.at[slot, f, source],
            device_id=(wide, source),
            device_id_type=pl.DeviceIdType.MESH,
        )

    def return_copy(slot, f, d):
        dest = lax.rem(me + d, narrow_count)
        return pltpu.make_async_remote_copy(
            src_ref=finished.at[slot, f, dest],
            dst_ref=returned.at[slot, f, me],
            send_sem=return_send.at[slot, f, d],
            recv_sem=return_recv.at[slot, f, me],
            device_id=(sides[slot], dest),
            device_id_type=pl.DeviceIdType.MESH,
        )

    def return_arrival(slot, f, d):
        source = lax.rem(me + d, narrow_count)
        return pltpu.make_async_remote_copy(
            src_ref=finished.at[slot, f, source],
            dst_ref=returned.at[slot, f, source],
            send_sem=return_send.at[slot, f, d],
            recv_sem=return_recv.at[slot, f, source],
            device_id=(sides[slot], source),
            device_id_type=pl.DeviceIdType.MESH,
        )

    own = pltpu.make_async_copy(x_ref.at[side], amps.at[0], own_sem)
    own.start()
    barrier = pltpu.get_barrier_semaphore()
    for slot in range(2):
        for d in range(1 - slot, narrow_count):
            peer = lax.rem(me + d, narrow_count)
            pl.semaphore_signal(
                barrier, inc=1, device_id=(sides[slot], peer), device_id_type=pl.DeviceIdType.MESH
            )
    pl.semaphore_wait(barrier, 2 * narrow_count - 1)
    window = min(2, chunk_count)
    for c in range(window):
        swap(c).start()

    cos_low, sin_low = phase_ref[0:1, :], phase_ref[3:4, :]
    re, im = gates_ref[0, 0].T, gates_ref[0, 1].T
    re, im = re * cos_low - im * sin_low, re * sin_low + im * cos_low
    upper = jnp.concatenate([re, im], axis=1)
    lower = jnp.concatenate([-im, re], axis=1)
    lane_gate = split(jnp.concatenate([upper, lower], axis=0))

    cos_mid = jnp.broadcast_to(phase_ref[1:2, :], (GATE, GATE)).T
    sin_mid = jnp.broadcast_to(phase_ref[4:5, :], (GATE, GATE)).T
    re, im = gates_ref[1, 0], gates_ref[1, 1]
    gate_rows[0] = re * cos_mid - im * sin_mid
    gate_rows[1] = re * sin_mid + im * cos_mid

    def row_start(s):
        return (s // low) * low * inner + s % low

    settings = GATE // inner
    re, im = [
        jnp.concatenate(
            [gate_rows[p, pl.ds(row_start(s), inner, stride=low), :] for s in range(settings)], axis=0
        )
        for p in range(2)
    ]
    row_gate = split(real_form(re, im))

    lanes = lax.broadcasted_iota(jnp.int32, (1, GATE), 1)

    def first_gates(slot, c):
        x = jnp.concatenate([amps[slot, c, pl.ds(p, GATE, stride=2), :] for p in range(2)], axis=0)
        y = product(row_gate, split(x))
        y = jnp.concatenate([y[:GATE], y[GATE:]], axis=1)
        y = product(split(y), lane_gate)
        re, im = y[:, :GATE], y[:, GATE:]
        device = sides[slot] * narrow_count + me
        top = ((device * 2 + side) * chunk_count + c) // top_span
        cos_top = jnp.sum(jnp.where(lanes == top, phase_ref[2:3, :], 0.0), axis=1, keepdims=True)
        sin_top = jnp.sum(jnp.where(lanes == top, phase_ref[5:6, :], 0.0), axis=1, keepdims=True)
        f, e = c // extra, c % extra
        shape = (narrow_count, per_dest * inner, GATE)
        spread[slot, f, :, e, 0] = (re * cos_top - im * sin_top).reshape(shape)
        spread[slot, f, :, e, 1] = (re * sin_top + im * cos_top).reshape(shape)
        if e == extra - 1:
            for d in range(1, narrow_count):
                spread_copy(slot, f, d).start()
            gathered[slot, f, me] = spread[slot, f, me]

    own.wait()
    for c in range(chunk_count):
        first_gates(0, c)

    third_gate = split(real_form(gates_ref[2, 0], gates_ref[2, 1]))

    def by_side(gate):
        turned = jnp.concatenate([gate[:, half:], gate[:, :half]], axis=1)
        turned = jnp.concatenate([turned[half:], turned[:half]], axis=0)
        return jnp.where(side == 0, gate, turned)

    fourth_gate = split(real_form(by_side(gates_ref[3, 0]), by_side(gates_ref[3, 1])))

    def last_gates(f):
        ys = []
        for slot in range(2):
            for d in range(1, narrow_count):
                spread_arrival(slot, f, d).wait_recv()
            columns = [
                jnp.concatenate(
                    [
                        gathered[slot, f, n, e, p, u * inner : (u + 1) * inner, :]
                        for p in range(2)
                        for n in range(narrow_count)
                        for e in range(extra)
                    ],
                    axis=0,
                )
                for u in range(per_dest)
            ]
            x = jnp.concatenate(columns, axis=1) if per_dest > 1 else columns[0]
            ys.append(product(third_gate, split(x)))
        for t in range(2):
            x = jnp.concatenate(
                [
                    ys[slot][p * GATE + t * half : p * GATE + (t + 1) * half]
                    for p in range(2)
                    for slot in range(2)
                ],
                axis=0,
            )
            z = product(fourth_gate, split(x))
            for slot in range(2):
                for n in range(narrow_count // 2):
                    for e in range(extra):
                        for p in range(2):
                            row = p * GATE + slot * half + (n * extra + e) * inner
                            for u in range(per_dest):
                                finished[
                                    slot, f, t * (narrow_count // 2) + n, e, p, u * inner : (u + 1) * inner, :
                                ] = z[row : row + inner, u * GATE : (u + 1) * GATE]
        for slot in (1, 0):
            for d in range(1 - slot, narrow_count):
                return_copy(slot, f, d).start()
        returned[0, f, me] = finished[0, f, me]

    for c in range(chunk_count):
        swap(c).wait_recv()
        if c + window < chunk_count:
            swap(c + window).start()
        first_gates(1, c)
        if c % extra == extra - 1:
            last_gates(c // extra)

    for f in range(free):
        for slot in range(2):
            for d in range(1 - slot, narrow_count):
                return_arrival(slot, f, d).wait_recv()
            origin = side if slot == 0 else 1 - side
            for n in range(narrow_count):
                for e in range(extra):
                    for p in range(2):
                        for u in range(per_dest):
                            row = 2 * row_start(n * per_dest + u) + p
                            out_ref[origin, f * extra + e, pl.ds(row, inner, stride=2 * low), :] = returned[
                                slot, f, n, e, p, u * inner : (u + 1) * inner, :
                            ]

    for c in range(chunk_count):
        swap(c).wait_send()
    for f in range(free):
        for slot in range(2):
            for d in range(1, narrow_count):
                spread_copy(slot, f, d).wait_send()
            for d in range(1 - slot, narrow_count):
                return_copy(slot, f, d).wait_send()


def local(state, gates, phase_index):
    local_amps = state.shape[1]
    narrow_count = lax.axis_size("narrow")
    wide_count = lax.axis_size("wide")
    rows = local_amps // GATE
    low = rows // GATE
    chunk_count = local_amps // (2 * GATE * GATE)
    contracted = GATE // narrow_count
    inner = min(contracted, GATE // low)
    extra = contracted // inner
    free = chunk_count // extra
    per_dest = GATE // inner // narrow_count
    top_span = local_amps * wide_count * narrow_count // GATE**3
    dims = (wide_count, narrow_count, chunk_count, free, extra, inner, low, per_dest, top_span)
    angles = phase_index.astype(jnp.float32) * angle_step
    phases = jnp.concatenate([jnp.cos(angles), jnp.sin(angles)], axis=0)
    x = state.reshape(2, rows, GATE).transpose(1, 0, 2).reshape(2, chunk_count, 2 * GATE, GATE)
    vmem = pl.BlockSpec(memory_space=pltpu.VMEM)
    message = pltpu.VMEM((2, free, narrow_count, extra, 2, per_dest * inner, GATE), jnp.float32)
    pair_sems = pltpu.SemaphoreType.DMA((2, free, narrow_count))
    flops = 4 * 2 * (2 * GATE) ** 2 * rows * 3
    out = pl.pallas_call(
        functools.partial(kernel, dims),
        out_shape=jax.ShapeDtypeStruct(x.shape, jnp.float32),
        in_specs=[pl.BlockSpec(memory_space=pl.ANY), vmem, vmem],
        out_specs=vmem,
        scratch_shapes=[
            pltpu.VMEM(x.shape, jnp.float32),
            pltpu.VMEM((2, GATE, GATE), jnp.float32),
            message,
            message,
            message,
            message,
            pltpu.SemaphoreType.DMA,
            pltpu.SemaphoreType.DMA((chunk_count,)),
            pltpu.SemaphoreType.DMA((chunk_count,)),
            pair_sems,
            pair_sems,
            pair_sems,
            pair_sems,
        ],
        compiler_params=pltpu.CompilerParams(
            collective_id=0, has_side_effects=True, vmem_limit_bytes=32 * 2**20
        ),
        cost_estimate=pl.CostEstimate(flops=flops, bytes_accessed=4 * local_amps * 4, transcendentals=0),
    )(x, gates, phases)
    return out.reshape(rows, 2, GATE).transpose(1, 0, 2).reshape(2, local_amps)


def solution(mesh):
    in_specs = (P(None, ("wide", "narrow")), P(), P())
    out_specs = P(None, ("wide", "narrow"))
    return jax.shard_map(local, mesh=mesh, in_specs=in_specs, out_specs=out_specs, check_vma=False)
```

time: 96.1 us -> 61.5 us (0.64)
  the two profiles are of different devices: /device:TPU:0 before, /device:TPU:12 now
where the time goes in v1:
time: 61.5 us; the launch traced here: 61.3 us
  Pallas kernels  57.3 us (93%)
  local copies, waits for them, and re-layouts  3.23 us (5%)
  other arithmetic  0.73 us (1%)
    pallas_call x1, Pallas kernels, local(): pl.pallas_call(functools.partial(kernel, dims), out_shape=jax.ShapeDtypeS...  57.3 us
    unnamed x5, local copies, waits for them, and re-layouts  3.23 us

profile of v1, /device:TPU:12, one launch (start us, length us, event | category | flops | bytes accessed | tf_op | source)
XLA Modules:
  0.0 61.3 jit_solution(12637445299673300292)
XLA Ops:
  0.0 0.7 %fusion.1 = (f32[3,128]{1,0:T(4,128)S(1)}, f32[3,128]{1,0:T(4,128)S(1)}) fusion(s32[3,128]{1,0:T(4,128)} %param.5), kind=kLoop, calls=%fused_computation.3 | loop fusion | flops 768 | bytes 4608 | tf_op jit(solution)/shard_map/cos | solution.py:279
  0.7 0.0 copy-start
  0.8 1.2 %copy-done = f32[2,131072]{1,0:T(2,128)S(1)} copy-done((f32[2,131072]{1,0:T(2,128)S(1)}, f32[2,131072]{1,0:T(2,128)}, u32[]{:S(2)}) %copy-start) | copy-done | bytes 1048600
  2.0 0.0 copy-start.1
  2.0 1.0 %copy-done.1 = f32[4,2,128,128]{3,2,1,0:T(8,128)S(1)} copy-done((f32[4,2,128,128]{3,2,1,0:T(8,128)S(1)}, f32[4,2,128,128]{3,2,1,0:T(8,128)}, u32[]{:S(2)}) %copy-start.1) | copy-done | bytes 524312
  3.0 57.3 %shard_map.37 = f32[2,4,256,128]{3,2,1,0:T(8,128)S(1)} custom-call(f32[2,4,256,128]{3,2,1,0:T(8,128)S(1)} %bitcast.11, f32[4,2,128,128]{3,2,1,0:T(8,128)S(1)} %copy-done.1, f32[6,128]{1,0:T(8,128)S(1)} %pad_maximum_fusion.phase_ref), custom_call_target="tpu_custom_call" | custom-call | flops 1610612736 | bytes 2097152 | tf_op jit(solution)/shard_map/pallas_call | solution.py:285
  60.3 1.0 %copy.7 = f32[2,131072]{1,0:T(2,128)} copy(f32[2,131072]{1,0:T(2,128)S(1)} %bitcast.10) | data formatting | bytes 2097152
  (1 shorter events, 0.0 us)
Async XLA Ops:
  0.7 1.2 %copy-start = (f32[2,131072]{1,0:T(2,128)S(1)}, f32[2,131072]{1,0:T(2,128)}, u32[]{:S(2)}) copy-start(f32[2,131072]{1,0:T(2,128)} %param.3) | copy-start | bytes 3145732
  2.0 1.0 %copy-start.1 = (f32[4,2,128,128]{3,2,1,0:T(8,128)S(1)}, f32[4,2,128,128]{3,2,1,0:T(8,128)}, u32[]{:S(2)}) copy-start(f32[4,2,128,128]{3,2,1,0:T(8,128)} %gates_ref.1) | copy-start | bytes 1572868

commit v2 on v1

--- a/solution.py
+++ b/solution.py
@@ -34,22 +34,25 @@
 def kernel(
     dims,
     x_ref,
-    gates_ref,
-    phase_ref,
+    gates_in,
+    phase_index_ref,
     out_ref,
     amps,
+    gates_ref,
     gate_rows,
     spread,
     gathered,
     finished,
     returned,
     own_sem,
+    gates_sem,
     swap_send,
     swap_recv,
     spread_send,
     spread_recv,
     return_send,
     return_recv,
+    credit,
 ):
     wide_count, narrow_count, chunk_count, free, extra, inner, low, per_dest, top_span = dims
     wide = lax.axis_index("wide")
@@ -57,6 +60,8 @@
     side = wide // (wide_count // 2)
     partner = lax.rem(wide + wide_count // 2, wide_count)
     sides = (wide, partner)
+    quarter = wide_count // 4
+    cross = wide + quarter * (1 - 2 * lax.rem(wide // quarter, 2))
     half = GATE // 2
 
     def swap(c):
@@ -115,6 +120,8 @@
 
     own = pltpu.make_async_copy(x_ref.at[side], amps.at[0], own_sem)
     own.start()
+    gates_copy = pltpu.make_async_copy(gates_in, gates_ref, gates_sem)
+    gates_copy.start()
     barrier = pltpu.get_barrier_semaphore()
     for slot in range(2):
         for d in range(1 - slot, narrow_count):
@@ -122,20 +129,25 @@
             pl.semaphore_signal(
                 barrier, inc=1, device_id=(sides[slot], peer), device_id_type=pl.DeviceIdType.MESH
             )
-    pl.semaphore_wait(barrier, 2 * narrow_count - 1)
+    pl.semaphore_signal(barrier, inc=1, device_id=(cross, me), device_id_type=pl.DeviceIdType.MESH)
+    pl.semaphore_wait(barrier, 2 * narrow_count)
     window = min(2, chunk_count)
     for c in range(window):
         swap(c).start()
 
-    cos_low, sin_low = phase_ref[0:1, :], phase_ref[3:4, :]
+    angles = phase_index_ref[...].astype(jnp.float32) * angle_step
+    cosine, sine = jnp.cos(angles), jnp.sin(angles)
+    gates_copy.wait()
+
+    cos_low, sin_low = cosine[0:1, :], sine[0:1, :]
     re, im = gates_ref[0, 0].T, gates_ref[0, 1].T
     re, im = re * cos_low - im * sin_low, re * sin_low + im * cos_low
     upper = jnp.concatenate([re, im], axis=1)
     lower = jnp.concatenate([-im, re], axis=1)
     lane_gate = split(jnp.concatenate([upper, lower], axis=0))
 
-    cos_mid = jnp.broadcast_to(phase_ref[1:2, :], (GATE, GATE)).T
-    sin_mid = jnp.broadcast_to(phase_ref[4:5, :], (GATE, GATE)).T
+    cos_mid = jnp.broadcast_to(cosine[1:2, :], (GATE, GATE)).T
+    sin_mid = jnp.broadcast_to(sine[1:2, :], (GATE, GATE)).T
     re, im = gates_ref[1, 0], gates_ref[1, 1]
     gate_rows[0] = re * cos_mid - im * sin_mid
     gate_rows[1] = re * sin_mid + im * cos_mid
@@ -162,8 +174,8 @@
         re, im = y[:, :GATE], y[:, GATE:]
         device = sides[slot] * narrow_count + me
         top = ((device * 2 + side) * chunk_count + c) // top_span
-        cos_top = jnp.sum(jnp.where(lanes == top, phase_ref[2:3, :], 0.0), axis=1, keepdims=True)
-        sin_top = jnp.sum(jnp.where(lanes == top, phase_ref[5:6, :], 0.0), axis=1, keepdims=True)
+        cos_top = jnp.sum(jnp.where(lanes == top, cosine[2:3, :], 0.0), axis=1, keepdims=True)
+        sin_top = jnp.sum(jnp.where(lanes == top, sine[2:3, :], 0.0), axis=1, keepdims=True)
         f, e = c // extra, c % extra
         shape = (narrow_count, per_dest * inner, GATE)
         spread[slot, f, :, e, 0] = (re * cos_top - im * sin_top).reshape(shape)
@@ -224,18 +236,29 @@
                                 finished[
                                     slot, f, t * (narrow_count // 2) + n, e, p, u * inner : (u + 1) * inner, :
                                 ] = z[row : row + inner, u * GATE : (u + 1) * GATE]
-        for slot in (1, 0):
-            for d in range(1 - slot, narrow_count):
-                return_copy(slot, f, d).start()
+        for d in range(1, narrow_count):
+            return_copy(0, f, d).start()
         returned[0, f, me] = finished[0, f, me]
 
+    waiting = []
     for c in range(chunk_count):
         swap(c).wait_recv()
-        if c + window < chunk_count:
-            swap(c + window).start()
+        last = c == chunk_count - 1
+        if not last:
+            pl.semaphore_signal(credit, inc=1, device_id=(cross, me), device_id_type=pl.DeviceIdType.MESH)
         first_gates(1, c)
+        if not last:
+            pl.semaphore_wait(credit, 1)
+            if c + window < chunk_count:
+                swap(c + window).start()
         if c % extra == extra - 1:
             last_gates(c // extra)
+            waiting.append(c // extra)
+        if c >= chunk_count - 2:
+            for f in waiting:
+                for d in range(narrow_count):
+                    return_copy(1, f, d).start()
+            waiting = []
 
     for f in range(free):
         for slot in range(2):
@@ -275,25 +298,26 @@
     per_dest = GATE // inner // narrow_count
     top_span = local_amps * wide_count * narrow_count // GATE**3
     dims = (wide_count, narrow_count, chunk_count, free, extra, inner, low, per_dest, top_span)
-    angles = phase_index.astype(jnp.float32) * angle_step
-    phases = jnp.concatenate([jnp.cos(angles), jnp.sin(angles)], axis=0)
     x = state.reshape(2, rows, GATE).transpose(1, 0, 2).reshape(2, chunk_count, 2 * GATE, GATE)
     vmem = pl.BlockSpec(memory_space=pltpu.VMEM)
+    hbm = pl.BlockSpec(memory_space=pltpu.HBM)
     message = pltpu.VMEM((2, free, narrow_count, extra, 2, per_dest * inner, GATE), jnp.float32)
     pair_sems = pltpu.SemaphoreType.DMA((2, free, narrow_count))
     flops = 4 * 2 * (2 * GATE) ** 2 * rows * 3
     out = pl.pallas_call(
         functools.partial(kernel, dims),
         out_shape=jax.ShapeDtypeStruct(x.shape, jnp.float32),
-        in_specs=[pl.BlockSpec(memory_space=pl.ANY), vmem, vmem],
+        in_specs=[hbm, hbm, vmem],
         out_specs=vmem,
         scratch_shapes=[
             pltpu.VMEM(x.shape, jnp.float32),
+            pltpu.VMEM(gates.shape, jnp.float32),
             pltpu.VMEM((2, GATE, GATE), jnp.float32),
             message,
             message,
             message,
             message,
+            pltpu.SemaphoreType.DMA,
             pltpu.SemaphoreType.DMA,
             pltpu.SemaphoreType.DMA((chunk_count,)),
             pltpu.SemaphoreType.DMA((chunk_count,)),
@@ -301,12 +325,13 @@
             pair_sems,
             pair_sems,
             pair_sems,
+            pltpu.SemaphoreType.REGULAR,
         ],
         compiler_params=pltpu.CompilerParams(
-            collective_id=0, has_side_effects=True, vmem_limit_bytes=32 * 2**20
+            collective_id=0, has_side_effects=True, vmem_limit_bytes=60 * 2**20
         ),
         cost_estimate=pl.CostEstimate(flops=flops, bytes_accessed=4 * local_amps * 4, transcendentals=0),
-    )(x, gates, phases)
+    )(x, gates, phase_index)
     return out.reshape(rows, 2, GATE).transpose(1, 0, 2).reshape(2, local_amps)
 
 

time: 61.5 us -> 61.6 us (level)
  the two profiles are of different devices: /device:TPU:12 before, /device:TPU:0 now
where the time goes in v2:
time: 61.6 us; the launch traced here: 61.4 us
  Pallas kernels  59.1 us (96%)
  local copies, waits for them, and re-layouts  2.26 us (4%)
    pallas_call x1, Pallas kernels, local(): pl.pallas_call(functools.partial(kernel, dims), out_shape=jax.ShapeDtypeS...  59.1 us
    unnamed x1, local copies, waits for them, and re-layouts  2.26 us

profile of v2, /device:TPU:0, one launch (start us, length us, event | category | flops | bytes accessed | tf_op | source)
XLA Modules:
  0.0 61.4 jit_solution(17049635905995911566)
XLA Ops:
  0.0 59.1 %shard_map.37 = f32[2,4,256,128]{3,2,1,0:T(8,128)} custom-call(f32[2,4,256,128]{3,2,1,0:T(8,128)} %bitcast.11, f32[4,2,128,128]{3,2,1,0:T(8,128)} %gates_in.1, s32[3,128]{1,0:T(4,128)} %phase_index_ref.1), custom_call_target="tpu_custom_call" | custom-call | flops 1610612736 | bytes 2097152 | tf_op jit(solution)/shard_map/pallas_call | solution.py:307
  59.1 2.3 %copy.7 = f32[2,131072]{1,0:T(2,128)} copy(f32[2,131072]{1,0:T(2,128)} %bitcast.10) | data formatting | bytes 2097152

commit v3 on v2

--- a/solution.py
+++ b/solution.py
@@ -52,7 +52,6 @@
     spread_recv,
     return_send,
     return_recv,
-    credit,
 ):
     wide_count, narrow_count, chunk_count, free, extra, inner, low, per_dest, top_span = dims
     wide = lax.axis_index("wide")
@@ -60,8 +59,6 @@
     side = wide // (wide_count // 2)
     partner = lax.rem(wide + wide_count // 2, wide_count)
     sides = (wide, partner)
-    quarter = wide_count // 4
-    cross = wide + quarter * (1 - 2 * lax.rem(wide // quarter, 2))
     half = GATE // 2
 
     def swap(c):
@@ -129,9 +126,8 @@
             pl.semaphore_signal(
                 barrier, inc=1, device_id=(sides[slot], peer), device_id_type=pl.DeviceIdType.MESH
             )
-    pl.semaphore_signal(barrier, inc=1, device_id=(cross, me), device_id_type=pl.DeviceIdType.MESH)
-    pl.semaphore_wait(barrier, 2 * narrow_count)
-    window = min(2, chunk_count)
+    pl.semaphore_wait(barrier, 2 * narrow_count - 1)
+    window = min(3, chunk_count)
     for c in range(window):
         swap(c).start()
 
@@ -186,7 +182,7 @@
             gathered[slot, f, me] = spread[slot, f, me]
 
     own.wait()
-    for c in range(chunk_count):
+    for c in range(extra):
         first_gates(0, c)
 
     third_gate = split(real_form(gates_ref[2, 0], gates_ref[2, 1]))
@@ -236,29 +232,22 @@
                                 finished[
                                     slot, f, t * (narrow_count // 2) + n, e, p, u * inner : (u + 1) * inner, :
                                 ] = z[row : row + inner, u * GATE : (u + 1) * GATE]
-        for d in range(1, narrow_count):
-            return_copy(0, f, d).start()
+        for slot in (1, 0):
+            for d in range(1 - slot, narrow_count):
+                return_copy(slot, f, d).start()
         returned[0, f, me] = finished[0, f, me]
 
-    waiting = []
-    for c in range(chunk_count):
-        swap(c).wait_recv()
-        last = c == chunk_count - 1
-        if not last:
-            pl.semaphore_signal(credit, inc=1, device_id=(cross, me), device_id_type=pl.DeviceIdType.MESH)
-        first_gates(1, c)
-        if not last:
-            pl.semaphore_wait(credit, 1)
+    for f in range(free):
+        if f > 0:
+            for e in range(extra):
+                first_gates(0, f * extra + e)
+        for e in range(extra):
+            c = f * extra + e
+            swap(c).wait_recv()
             if c + window < chunk_count:
                 swap(c + window).start()
-        if c % extra == extra - 1:
-            last_gates(c // extra)
-            waiting.append(c // extra)
-        if c >= chunk_count - 2:
-            for f in waiting:
-                for d in range(narrow_count):
-                    return_copy(1, f, d).start()
-            waiting = []
+            first_gates(1, c)
+        last_gates(f)
 
     for f in range(free):
         for slot in range(2):
@@ -325,7 +314,6 @@
             pair_sems,
             pair_sems,
             pair_sems,
-            pltpu.SemaphoreType.REGULAR,
         ],
         compiler_params=pltpu.CompilerParams(
             collective_id=0, has_side_effects=True, vmem_limit_bytes=60 * 2**20

time: 61.6 us -> 55.4 us (0.90)
  the two profiles are of different devices: /device:TPU:0 before, /device:TPU:25 now
where the time goes in v3:
time: 55.4 us; the launch traced here: 55.2 us
  Pallas kernels  52.9 us (95%)
  local copies, waits for them, and re-layouts  2.26 us (4%)
    pallas_call x1, Pallas kernels, local(): pl.pallas_call(functools.partial(kernel, dims), out_shape=jax.ShapeDtypeS...  52.9 us
    unnamed x1, local copies, waits for them, and re-layouts  2.26 us

profile of v3, /device:TPU:25, one launch (start us, length us, event | category | flops | bytes accessed | tf_op | source)
XLA Modules:
  0.0 55.2 jit_solution(4383944578939538760)
XLA Ops:
  0.0 52.9 %shard_map.37 = f32[2,4,256,128]{3,2,1,0:T(8,128)} custom-call(f32[2,4,256,128]{3,2,1,0:T(8,128)} %bitcast.11, f32[4,2,128,128]{3,2,1,0:T(8,128)} %gates_in.1, s32[3,128]{1,0:T(4,128)} %phase_index_ref.1), custom_call_target="tpu_custom_call" | custom-call | flops 1610612736 | bytes 2097152 | tf_op jit(solution)/shard_map/pallas_call | solution.py:296
  52.9 2.3 %copy.7 = f32[2,131072]{1,0:T(2,128)} copy(f32[2,131072]{1,0:T(2,128)} %bitcast.10) | data formatting | bytes 2097152

commit v4 on v3

--- a/solution.py
+++ b/solution.py
@@ -46,6 +46,8 @@
     returned,
     own_sem,
     gates_sem,
+    staged,
+    out_sem,
     swap_send,
     swap_recv,
     spread_send,
@@ -249,6 +251,11 @@
             first_gates(1, c)
         last_gates(f)
 
+    def store(slot, f):
+        origin = side if slot == 0 else 1 - side
+        part = pl.ds(f * extra, extra)
+        return pltpu.make_async_copy(staged.at[origin, part], out_ref.at[origin, part], out_sem.at[f, slot])
+
     for f in range(free):
         for slot in range(2):
             for d in range(1 - slot, narrow_count):
@@ -259,9 +266,11 @@
                     for p in range(2):
                         for u in range(per_dest):
                             row = 2 * row_start(n * per_dest + u) + p
-                            out_ref[origin, f * extra + e, pl.ds(row, inner, stride=2 * low), :] = returned[
+                            staged[origin, f * extra + e, pl.ds(row, inner, stride=2 * low), :] = returned[
                                 slot, f, n, e, p, u * inner : (u + 1) * inner, :
                             ]
+
+            store(slot, f).start()
 
     for c in range(chunk_count):
         swap(c).wait_send()
@@ -271,6 +280,7 @@
                 spread_copy(slot, f, d).wait_send()
             for d in range(1 - slot, narrow_count):
                 return_copy(slot, f, d).wait_send()
+            store(slot, f).wait()
 
 
 def local(state, gates, phase_index):
@@ -297,7 +307,7 @@
         functools.partial(kernel, dims),
         out_shape=jax.ShapeDtypeStruct(x.shape, jnp.float32),
         in_specs=[hbm, hbm, vmem],
-        out_specs=vmem,
+        out_specs=hbm,
         scratch_shapes=[
             pltpu.VMEM(x.shape, jnp.float32),
             pltpu.VMEM(gates.shape, jnp.float32),
@@ -308,6 +318,8 @@
             message,
             pltpu.SemaphoreType.DMA,
             pltpu.SemaphoreType.DMA,
+            pltpu.VMEM(x.shape, jnp.float32),
+            pltpu.SemaphoreType.DMA((free, 2)),
             pltpu.SemaphoreType.DMA((chunk_count,)),
             pltpu.SemaphoreType.DMA((chunk_count,)),
             pair_sems,

time: 55.4 us -> 55.1 us (level)
  no operation moved by 1% of the time
where the time goes in v4:
time: 55.1 us; the launch traced here: 54.9 us
  Pallas kernels  52.6 us (95%)
  local copies, waits for them, and re-layouts  2.26 us (4%)
    pallas_call x1, Pallas kernels, local(): pl.pallas_call(functools.partial(kernel, dims), out_shape=jax.ShapeDtypeS...  52.6 us
    unnamed x1, local copies, waits for them, and re-layouts  2.26 us

profile of v4, /device:TPU:25, one launch (start us, length us, event | category | flops | bytes accessed | tf_op | source)
XLA Modules:
  0.0 54.9 jit_solution(1898230624564327588)
XLA Ops:
  0.0 52.6 %shard_map.37 = f32[2,4,256,128]{3,2,1,0:T(8,128)} custom-call(f32[2,4,256,128]{3,2,1,0:T(8,128)} %bitcast.11, f32[4,2,128,128]{3,2,1,0:T(8,128)} %gates_in.1, s32[3,128]{1,0:T(4,128)} %phase_index_ref.1), custom_call_target="tpu_custom_call" | custom-call | flops 1610612736 | bytes 2097152 | tf_op jit(solution)/shard_map/pallas_call | solution.py:306
  52.6 2.3 %copy.7 = f32[2,131072]{1,0:T(2,128)} copy(f32[2,131072]{1,0:T(2,128)} %bitcast.10) | data formatting | bytes 2097152

commit v5 on v4

--- a/solution.py
+++ b/solution.py
@@ -73,24 +73,24 @@
             device_id_type=pl.DeviceIdType.MESH,
         )
 
-    def spread_copy(slot, f, d):
+    def spread_copy(slot, f, e, d):
         dest = lax.rem(me + d, narrow_count)
         return pltpu.make_async_remote_copy(
-            src_ref=spread.at[slot, f, dest],
-            dst_ref=gathered.at[slot, f, me],
-            send_sem=spread_send.at[slot, f, d],
-            recv_sem=spread_recv.at[slot, f, me],
+            src_ref=spread.at[slot, f, dest, e],
+            dst_ref=gathered.at[slot, f, me, e],
+            send_sem=spread_send.at[slot, f, e, d],
+            recv_sem=spread_recv.at[slot, f, e, me],
             device_id=(wide, dest),
             device_id_type=pl.DeviceIdType.MESH,
         )
 
-    def spread_arrival(slot, f, d):
+    def spread_arrival(slot, f, e, d):
         source = lax.rem(me + d, narrow_count)
         return pltpu.make_async_remote_copy(
-            src_ref=spread.at[slot, f, source],
-            dst_ref=gathered.at[slot, f, source],
-            send_sem=spread_send.at[slot, f, d],
-            recv_sem=spread_recv.at[slot, f, source],
+            src_ref=spread.at[slot, f, source, e],
+            dst_ref=gathered.at[slot, f, source, e],
+            send_sem=spread_send.at[slot, f, e, d],
+            recv_sem=spread_recv.at[slot, f, e, source],
             device_id=(wide, source),
             device_id_type=pl.DeviceIdType.MESH,
         )
@@ -178,10 +178,9 @@
         shape = (narrow_count, per_dest * inner, GATE)
         spread[slot, f, :, e, 0] = (re * cos_top - im * sin_top).reshape(shape)
         spread[slot, f, :, e, 1] = (re * sin_top + im * cos_top).reshape(shape)
-        if e == extra - 1:
-            for d in range(1, narrow_count):
-                spread_copy(slot, f, d).start()
-            gathered[slot, f, me] = spread[slot, f, me]
+        for d in range(1, narrow_count):
+            spread_copy(slot, f, e, d).start()
+        gathered[slot, f, me, e] = spread[slot, f, me, e]
 
     own.wait()
     for c in range(extra):
@@ -200,7 +199,8 @@
         ys = []
         for slot in range(2):
             for d in range(1, narrow_count):
-                spread_arrival(slot, f, d).wait_recv()
+                for e in range(extra):
+                    spread_arrival(slot, f, e, d).wait_recv()
             columns = [
                 jnp.concatenate(
                     [
@@ -277,7 +277,8 @@
     for f in range(free):
         for slot in range(2):
             for d in range(1, narrow_count):
-                spread_copy(slot, f, d).wait_send()
+                for e in range(extra):
+                    spread_copy(slot, f, e, d).wait_send()
             for d in range(1 - slot, narrow_count):
                 return_copy(slot, f, d).wait_send()
             store(slot, f).wait()
@@ -301,6 +302,7 @@
     vmem = pl.BlockSpec(memory_space=pltpu.VMEM)
     hbm = pl.BlockSpec(memory_space=pltpu.HBM)
     message = pltpu.VMEM((2, free, narrow_count, extra, 2, per_dest * inner, GATE), jnp.float32)
+    piece_sems = pltpu.SemaphoreType.DMA((2, free, extra, narrow_count))
     pair_sems = pltpu.SemaphoreType.DMA((2, free, narrow_count))
     flops = 4 * 2 * (2 * GATE) ** 2 * rows * 3
     out = pl.pallas_call(
@@ -322,8 +324,8 @@
             pltpu.SemaphoreType.DMA((free, 2)),
             pltpu.SemaphoreType.DMA((chunk_count,)),
             pltpu.SemaphoreType.DMA((chunk_count,)),
-            pair_sems,
-            pair_sems,
+            piece_sems,
+            piece_sems,
             pair_sems,
             pair_sems,
         ],

time: 55.1 us -> 56.9 us (1.033)
  the two profiles are of different devices: /device:TPU:25 before, /device:TPU:0 now
where the time goes in v5:
time: 56.9 us; the launch traced here: 56.8 us
  Pallas kernels  54.5 us (96%)
  local copies, waits for them, and re-layouts  2.26 us (4%)
    pallas_call x1, Pallas kernels, local(): pl.pallas_call(functools.partial(kernel, dims), out_shape=jax.ShapeDtypeS...  54.5 us
    unnamed x1, local copies, waits for them, and re-layouts  2.26 us

profile of v5, /device:TPU:0, one launch (start us, length us, event | category | flops | bytes accessed | tf_op | source)
XLA Modules:
  0.0 56.8 jit_solution(13152770279338095449)
XLA Ops:
  0.0 54.5 %shard_map.37 = f32[2,4,256,128]{3,2,1,0:T(8,128)} custom-call(f32[2,4,256,128]{3,2,1,0:T(8,128)} %bitcast.11, f32[4,2,128,128]{3,2,1,0:T(8,128)} %gates_in.1, s32[3,128]{1,0:T(4,128)} %phase_index_ref.1), custom_call_target="tpu_custom_call" | custom-call | flops 1610612736 | bytes 2097152 | tf_op jit(solution)/shard_map/pallas_call | solution.py:308
  54.5 2.3 %copy.7 = f32[2,131072]{1,0:T(2,128)} copy(f32[2,131072]{1,0:T(2,128)} %bitcast.10) | data formatting | bytes 2097152
